TPU v7x, 32 devices: a whole 2x2x4 slice. The times are simulated.
32 devices in a mesh: groups: 2 (over x), row: 16 (over z, y, core).
Axes of the slice: x: 2, y: 2, z: 4, core: 2. Of those that a mesh axis runs over, the one named last changes fastest.
Arguments:
- features: bfloat16 [8192, 256], P(('groups', 'row')), parts along dimension 0, may hold values from -6 to 6
- self_weight: bfloat16 [256, 256], replicated, may hold values from -0.375 to 0.375
- neigh_weight: bfloat16 [256, 256], replicated, may hold values from -3 to 3
- tile_vals: bfloat16 [64, 64, 128, 128], P(('groups', 'row')), parts along dimension 0, may hold values from 0 to 6, as said below
- tile_cols: int32 [64, 64], P(('groups', 'row')), parts along dimension 0, may hold values from 0 to 31, as said below
- tile_count: int32 [64], P(('groups', 'row')), parts along dimension 0, may hold values from 1 to 64, as said below
- pos_index: int32 [8192], P(('groups', 'row')), parts along dimension 0, may hold values from 0 to 4095
- neg_index: int32 [8192], P(('groups', 'row')), parts along dimension 0, may hold values from 0 to 4095
Outputs:
- loss: float32 [2], P('groups'), parts along dimension 0
- grad_self: float32 [512, 256], P('groups'), parts along dimension 0
- grad_neigh: float32 [512, 256], P('groups'), parts along dimension 0
- grad_feat: float32 [8192, 256], P(('groups', 'row')), parts along dimension 0
There are 2 independent parts, one for each index of `groups`. A program takes and returns all parts, laid end to end along the dimension named above; an argument that names none is the same for every part. Nothing has to cross between parts.
Inputs may be any that keep to these rules, and one draw needn't show every extreme that they name: `tile_vals`: Nonnegative; slot 0 of every row tile has a diagonal of 1 or more. `tile_cols`: slot 0 of row tile r holds column tile r. `tile_count`: some row tile has all 64 slots live.
All inputs are finite; a program needn't handle non-finite values.
Results may differ from a plain program's by a relative error of at most 0.0046.
Values may be sent and summed in bfloat16 or wider, within the bound.
A program may use at most 128 MiB of HBM per device.

v0:
```python
import jax
import jax.numpy as jnp
from jax import lax
from jax.sharding import PartitionSpec as P


def on_device(
    features, self_weight, neigh_weight, tile_vals, tile_cols, tile_count, pos_index, neg_index
):
    local_rows, width_f = features.shape
    tile_rows = tile_vals.shape[0]
    slot_count = tile_vals.shape[1]
    tile_size = tile_vals.shape[2]
    row_devices = lax.axis_size("row")
    node_count = local_rows * row_devices
    column_tiles = node_count // tile_size
    all_nodes = lax.all_gather(features, "row", axis=0, tiled=True)
    node_blocks = all_nodes.reshape(column_tiles, tile_size, width_f)
    live_slot = jnp.arange(slot_count)[None, :] < tile_count[:, None]
    masked = jnp.where(live_slot[:, :, None, None], tile_vals, jnp.zeros((), tile_vals.dtype))
    degree = jnp.sum(masked, axis=(1, 3), dtype=jnp.float32)
    picked = node_blocks[tile_cols]
    summed = jnp.einsum("rsij,rsjf->rif", masked, picked, preferred_element_type=jnp.float32)
    mean_near = (summed / degree[:, :, None]).reshape(local_rows, width_f).astype(jnp.bfloat16)
    pre = jnp.dot(features, self_weight, preferred_element_type=jnp.float32) + jnp.dot(
        mean_near, neigh_weight, preferred_element_type=jnp.float32
    )
    sig_pre = jax.nn.sigmoid(pre)
    hidden = pre * sig_pre
    inverse = 1.0 / jnp.sqrt(jnp.sum(hidden * hidden, axis=-1) + 1e-05)
    embed = hidden * inverse[:, None]
    pos_rows = all_nodes[pos_index].astype(jnp.float32)
    neg_rows = all_nodes[neg_index].astype(jnp.float32)
    score_pos = jnp.sum(embed * pos_rows, axis=-1)
    score_neg = jnp.sum(embed * neg_rows, axis=-1)
    loss_part = jnp.sum(jax.nn.softplus(-score_pos) + jax.nn.softplus(score_neg))
    d_embed = (-jax.nn.sigmoid(-score_pos))[:, None] * pos_rows + jax.nn.sigmoid(score_neg)[
        :, None
    ] * neg_rows
    d_hidden = inverse[:, None] * (
        d_embed - embed * jnp.sum(d_embed * embed, axis=-1, keepdims=True)
    )
    d_pre = (d_hidden * sig_pre * (1.0 + pre * (1.0 - sig_pre))).astype(jnp.bfloat16)
    scale = 1.0 / jnp.sqrt(jnp.float32(node_count))
    self_part = scale * jnp.dot(features.T, d_pre, preferred_element_type=jnp.float32)
    neigh_part = scale * jnp.dot(mean_near.T, d_pre, preferred_element_type=jnp.float32)
    grad_self, grad_neigh, loss_total = lax.psum((self_part, neigh_part, loss_part), "row")
    degree_rows = degree.reshape(local_rows)
    g_neigh = (
        jnp.dot(d_pre, neigh_weight.T, preferred_element_type=jnp.float32) / degree_rows[:, None]
    ).astype(jnp.bfloat16)
    g_blocks = g_neigh.reshape(tile_rows, tile_size, width_f)
    parts = jnp.einsum("rsij,rif->rsjf", masked, g_blocks, preferred_element_type=jnp.float32)
    column_total = (
        jnp.zeros((column_tiles, tile_size, width_f), jnp.float32)
        .at[tile_cols.reshape(-1)]
        .add(parts.reshape(-1, tile_size, width_f))
    )
    flat_total = column_total.reshape(node_count, width_f)
    spread_back = lax.psum_scatter(flat_total, "row", scatter_dimension=0, tiled=True)
    grad_feat = jnp.dot(d_pre, self_weight.T, preferred_element_type=jnp.float32) + spread_back
    loss = (loss_total / jnp.float32(node_count)).reshape(1)
    return (loss, grad_self, grad_neigh, grad_feat)


def solution(mesh):
    placed = (
        P(("groups", "row"), None),
        P(),
        P(),
        P(("groups", "row"), None, None, None),
        P(("groups", "row"), None),
        P(("groups", "row")),
        P(("groups", "row")),
        P(("groups", "row")),
    )
    return jax.shard_map(
        on_device,
        mesh=mesh,
        in_specs=placed,
        out_specs=(P("groups"), P("groups", None), P("groups", None), P(("groups", "row"), None)),
        check_vma=False,
    )
```

profile of v0, /device:TPU:0, one launch (start us, length us, event | category | flops | bytes accessed | tf_op | source)
XLA Modules:
  0.0 251.6 jit_solution(3396428478382689341)
XLA Ops:
  7.2 0.7 all-gather.2.cloned.1.call-update
  8.0 0.8 reshape.98
  8.7 0.7 compare_select_fusion.4
  9.5 0.7 compare_select_fusion.3
  10.2 0.7 compare_select_fusion.1
  10.9 0.7 iota_compare_fusion
  11.6 1.2 fusion.18
  12.8 3.3 %convert_reduce_fusion = f32[2,128]{1,0:T(2,128)S(1)} fusion(bf16[2,64,128,128]{3,2,1,0:T(8,128)(2,1)} %param.11, pred[2,64]{1,0:T(4,128)(4,1)S(1)} %iota_compare_fusion), kind=kLoop, calls=%fused_computation.4 | loop fusion | flops 6291200 | bytes 4195456 | tf_op jit(solution)/shard_map/reduce_sum | solution.py:21
  16.1 38.2 %all-gather.2.cloned.1.call-done = bf16[4096,256]{1,0:T(8,128)(2,1)} async-done(((bf16[256,256]{1,0:T(8,128)(2,1)}), bf16[4096,256]{1,0:T(8,128)(2,1)}) %all-gather.2.cloned.1.call-update) | async-done | bytes 2097168 | tf_op jit(solution)/shard_map/all_gather | solution.py:17
  54.3 8.2 %gather_fusion = bf16[128,128,256]{2,1,0:T(8,128)(2,1)} fusion(bf16[32,128,256]{2,1,0:T(8,128)(2,1)} %bitcast.39, s32[1024]{0:T(1024)S(1)} %pad_clamp_fusion.2), kind=kCustom, calls=%fused_computation | custom fusion | bytes 16777728 | tf_op jit(solution)/shard_map/gather | solution.py:22
  62.5 6.1 %fusion.8 = bf16[2,128,256]{2,1,0:T(8,128)(2,1)S(1)} fusion(bf16[2,64,128,256]{3,2,1,0:T(8,128)(2,1)} %bitcast.40, bf16[2,64,128,128]{3,2,1,0:T(8,128)(2,1)} %param.11, pred[2,64]{1,0:T(4,128)(4,1)S(1)} %iota_compare_fusion, f32[2,128]{1,0:T(2,128)S(1)} %convert_reduce_fusion), kind=kOutput, calls=%fused_computation.19 | convolution fusion | flops 1075970048 | bytes 12715136 | tf_op jit(solution)/shard_map/rsij,rsjf->rif/dot_general | solution.py:23
  68.6 0.3 multiply_reduce_fusion.1
  68.9 1.2 gather_fusion.1
  70.1 0.1 copy.12
  70.2 1.2 gather_fusion.2
  71.3 0.1 copy.13
  71.4 0.1 fusion.9
  71.6 0.6 divide_negate_fusion
  72.2 0.1 multiply_reduce_fusion
  72.3 0.2 multiply_convert_fusion
  72.5 0.9 convolution_multiply_fusion
  73.4 0.9 fusion.4
  74.3 0.2 fusion.6
  74.6 11.4 %fusion = f32[2,64,128,256]{3,2,1,0:T(8,128)} fusion(bf16[2,128,256,1]{2,1,3,0:T(8,128)(2,1)S(1)} %bitcast.41, bf16[2,64,128,128]{3,2,1,0:T(8,128)(2,1)} %param.11, pred[2,64]{1,0:T(4,128)(4,1)S(1)} %iota_compare_fusion), kind=kOutput, calls=%fused_computation.6 | convolution fusion | flops 1075838976 | bytes 21102720 | tf_op jit(solution)/shard_map/rsij,rif->rsjf/dot_general | solution.py:53
  86.0 2.4 broadcast_in_dim.39
  88.4 37.9 %scatter_fusion = f32[32,128,256]{2,1,0:T(8,128)} fusion(f32[32,128,256]{2,1,0:T(8,128)} %broadcast_in_dim.39, s32[128]{0:T(128)S(1)} %fusion.15, f32[128,128,256]{2,1,0:T(8,128)} %bitcast.38), kind=kCustom, calls=%fused_computation.3 | custom fusion | flops 4194304 | bytes 50332160 | tf_op jit(solution)/shard_map/scatter-add | solution.py:57
  126.3 32.3 %psum.21 = f32[]{:T(128)} all-reduce(f32[]{:T(128)} %get-tuple-element.13), channel_id=1, replica_groups=mesh['groups'=2,'row'=16] {'row'}, use_global_device_ids=true, to_apply=%region_5.6 | all-reduce | flops 1 | bytes 8 | tf_op jit(solution)/shard_map/psum | solution.py:47
  159.3 4.4 %all-reduce.3.cloned.1.call-done = (f32[256,256]{0,1:T(8,128)}, f32[256,256]{1,0:T(8,128)}) async-done(((f32[256,256]{0,1:T(8,128)}, f32[256,256]{1,0:T(8,128)}), (f32[256,256]{0,1:T(8,128)}, f32[256,256]{1,0:T(8,128)})) %all-reduce.3.cloned.1.call-update) | async-done | bytes 524304 | tf_op jit(solution)/shard_map/psum | solution.py:47
  163.6 1.8 copy.15
  165.4 74.9 %reduce-scatter.2.cloned.1.call-done = f32[256,256]{1,0:T(8,128)} async-done(((f32[4096,256]{1,0:T(8,128)}), f32[256,256]{1,0:T(8,128)}) %reduce-scatter.2.cloned.1.call-update) | async-done | bytes 262160 | tf_op jit(solution)/shard_map/reduce_scatter | solution.py:60
  240.4 1.9 convolution_add_fusion
  242.3 1.7 copy.22
  (19 shorter events, 0.3 us)
Async XLA Ops:
  7.2 61.4 %copy-start = (bf16[256,256]{1,0:T(8,128)(2,1)S(1)}, bf16[256,256]{1,0:T(8,128)(2,1)}, u32[]{:S(2)}) copy-start(bf16[256,256]{1,0:T(8,128)(2,1)} %param.10) | copy-start | bytes 393220
  7.2 47.1 %all-gather.2.cloned.1.call-start = ((), (), s32[]{:S(2)}) async-start(), calls=%async_computation.1 | async-start | bytes 2228224 | tf_op jit(solution)/shard_map/all_gather | solution.py:17
  7.9 155.7 %all-reduce.3.cloned.1.call-start = ((), (), s32[]{:S(2)}) async-start(), calls=%async_computation.3 | async-start | bytes 1048576 | tf_op jit(solution)/shard_map/psum | solution.py:47
  62.5 6.4 %copy-start.1 = (bf16[4096,256]{1,0:T(8,128)(2,1)S(1)}, bf16[4096,256]{1,0:T(8,128)(2,1)}, u32[]{:S(2)}) copy-start(bf16[4096,256]{1,0:T(8,128)(2,1)} %all-gather.2.cloned.1.call-done) | copy-start | bytes 6291460
  68.6 4.9 %copy-start.2 = (bf16[256,256]{1,0:T(8,128)(2,1)S(1)}, bf16[256,256]{1,0:T(8,128)(2,1)}, u32[]{:S(2)}) copy-start(bf16[256,256]{1,0:T(8,128)(2,1)} %param.8) | copy-start | bytes 393220
  74.6 165.8 %reduce-scatter.2.cloned.1.call-start = ((), (), s32[]{:S(2)}) async-start(), calls=%async_computation.2 | async-start | bytes 4456448 | tf_op jit(solution)/shard_map/reduce_scatter | solution.py:60
  126.3 114.1 %copy-start.3 = (bf16[256,256]{1,0:T(8,128)(2,1)S(1)}, bf16[256,256]{1,0:T(8,128)(2,1)}, u32[]{:S(2)}) copy-start(bf16[256,256]{1,0:T(8,128)(2,1)} %param.9) | copy-start | bytes 393220
Sparse Core Ops, SparseCore 0:
  10.2 44.0 all-gather.1
  74.7 88.9 all-reduce.2
  167.5 72.8 reduce-scatter.1
where the time goes:
time: 252 us
  waiting for transfers between devices  118 us (47%)
  other arithmetic  45 us (18%)
  blocking collectives  32.3 us (13%)
  matrix products  22.9 us (9%)
  local copies, waits for them, and re-layouts  17.4 us (7%)
  between operations  15.6 us (6%)
    reduce_scatter x1, waiting for transfers between devices, on_device(): lax.psum_scatter(flat_total, 'row', scatter_dimension=0, tiled=True)  74.9 us
    all_gather x1, waiting for transfers between devices, on_device(): all_nodes = lax.all_gather(features, 'row', axis=0, tiled=True)  38.2 us
    scatter-add x1, other arithmetic, on_device(): column_total = jnp.zeros((column_tiles, tile_size, width_f), jnp.float32)...  37.9 us
    psum x1, blocking collectives, on_device(): lax.psum((self_part, neigh_part, loss_part), 'row')  32.3 us
    dot_general x1, matrix products, on_device(): jnp.einsum('rsij,rif->rsjf', masked, g_blocks, preferred_element_type=jnp...  11.4 us
    gather x1, local copies, waits for them, and re-layouts, on_device(): picked = node_blocks[tile_cols]  8.15 us
    dot_general x1, matrix products, on_device(): jnp.einsum('rsij,rsjf->rif', masked, picked, preferred_element_type=jnp.f...  6.09 us
  transfers between devices with their start and end apart: 3, of which 3 were waited for; matrix products, arithmetic and copies ran while one was open for 24% of the time, Pallas kernels for 0%

commit v1 on v0

v1 whole, which is shorter than its diff:
```python
import functools

import jax
import jax.numpy as jnp
from jax import lax
from jax.experimental import pallas as pl
from jax.experimental.pallas import tpu as pltpu
from jax.sharding import PartitionSpec as P

F32 = jnp.float32
BF16 = jnp.bfloat16
MESH = pl.DeviceIdType.MESH
SLOT_BLOCK = 16


def dense_kernel(cols_ref, count_ref, tiles_ref, adj_ref, deg_ref, acc):
    r, b = pl.program_id(0), pl.program_id(1)
    block = tiles_ref.shape[1]
    column_tiles, tile, _ = acc.shape

    @pl.when(b == 0)
    def _():
        def clear(i, carry):
            acc[i] = jnp.zeros((tile, tile), F32)
            return carry

        lax.fori_loop(0, column_tiles, clear, 0)

    live = jnp.clip(count_ref[r] - b * block, 0, block)

    def add(i, carry):
        col = cols_ref[r, b * block + i]
        acc[col] += tiles_ref[0, i].astype(F32)
        return carry

    lax.fori_loop(0, live, add, 0)

    @pl.when(b == pl.num_programs(1) - 1)
    def _():
        def finish(p, total):
            left, right = acc[2 * p], acc[2 * p + 1]
            adj_ref[p, :, :tile] = left.astype(BF16)
            adj_ref[p, :, tile:] = right.astype(BF16)
            return total + left + right

        total = lax.fori_loop(0, column_tiles // 2, finish, jnp.zeros((tile, tile), F32))
        deg_ref[...] = jnp.broadcast_to(jnp.sum(total, axis=1, keepdims=True), (tile, tile))


def dense_rows(tile_vals, tile_cols, tile_count, shards):
    tile_rows, slots, tile, _ = tile_vals.shape
    block = SLOT_BLOCK if slots % SLOT_BLOCK == 0 else slots

    def tiles_at(r, b, cols, count):
        return (r, jnp.minimum(b, (count[r] - 1) // block), 0, 0)

    return pl.pallas_call(
        dense_kernel,
        grid_spec=pltpu.PrefetchScalarGridSpec(
            num_scalar_prefetch=2,
            grid=(tile_rows, slots // block),
            in_specs=[pl.BlockSpec((1, block, tile, tile), tiles_at)],
            out_specs=[
                pl.BlockSpec((shards, tile, 2 * tile), lambda r, b, cols, count: (0, r, 0)),
                pl.BlockSpec((tile, tile), lambda r, b, cols, count: (r, 0)),
            ],
            scratch_shapes=[pltpu.VMEM((2 * shards, tile, tile), F32)],
        ),
        out_shape=[
            jax.ShapeDtypeStruct((shards, tile_rows * tile, 2 * tile), BF16),
            jax.ShapeDtypeStruct((tile_rows * tile, tile), F32),
        ],
        compiler_params=pltpu.CompilerParams(vmem_limit_bytes=48 * 1024 * 1024),
    )(tile_cols, tile_count, tile_vals)


def layer_kernel(
    Z, x_ref, ws_ref, wn_ref, adj_ref, deg_ref, pos_ref, neg_ref,
    loss_ref, gself_ref, gneigh_ref, gfeat_ref,
    feats, adj, adj_p, idx, acc, dpre, mean,
    gnt, gn32, gfull, g_in, gy_out, gy_in, gz, gh, gp,
    l_own, l_core, l_sum, l_y, lz,
    y_out, y_in, z_out, up_in, dn_in,
    adj_sem, adjp_s, adjp_r, recv, up_s, dn_s, y_s, core_s,
    ex_s, ex_r, gz_s, gz_r, lz_s, lz_r, ys_s, ys_r, zs_s, up_r, dn_r,
):
    rows, width = x_ref.shape
    half = rows // 2
    me = lax.axis_index("row")
    z, y, c = me // 4, (me // 2) % 2, me % 2

    def dev(zz, yy, cc):
        return (zz * 2 + yy) * 2 + cc

    core_peer, y_peer = dev(z, y, 1 - c), dev(z, 1 - y, c)
    up_peer = dev(jnp.minimum(z + 1, Z - 1), y, c)
    dn_peer = dev(jnp.maximum(z - 1, 0), y, c)

    def remote(src, dst, ss, rs, target):
        return pltpu.make_async_remote_copy(
            src_ref=src, dst_ref=dst, send_sem=ss, recv_sem=rs,
            device_id={"row": target}, device_id_type=MESH,
        )

    adj_load = pltpu.make_async_copy(adj_ref, adj, adj_sem)
    adj_load.start()

    barrier = pltpu.get_barrier_semaphore()
    pl.semaphore_signal(barrier, inc=1, device_id={"row": core_peer}, device_id_type=MESH)
    pl.semaphore_signal(barrier, inc=1, device_id={"row": y_peer}, device_id_type=MESH)
    for k in range(1, Z):
        pl.semaphore_signal(
            barrier, inc=1, device_id={"row": dev((z + k) % Z, y, c)}, device_id_type=MESH
        )
    feats[me] = x_ref[...]
    pl.semaphore_wait(barrier, Z + 1)

    def go_up(zs):
        s = dev(zs, y, c)
        return remote(feats.at[s], feats.at[s], up_s.at[zs], recv.at[s], up_peer)

    def go_dn(zs):
        s = dev(zs, y, c)
        return remote(feats.at[s], feats.at[s], dn_s.at[zs], recv.at[s], dn_peer)

    def go_y(zs):
        s = dev(zs, y, c)
        return remote(feats.at[s], feats.at[s], y_s.at[zs], recv.at[s], y_peer)

    def go_core(zs, yy):
        s = dev(zs, yy, c)
        return remote(feats.at[s], feats.at[s], core_s.at[zs * 2 + yy], recv.at[s], core_peer)

    def arrived(s):
        remote(feats.at[s], feats.at[s], core_s.at[0], recv.at[s], core_peer).wait_recv()

    @pl.when(z < Z - 1)
    def _():
        go_up(z).start()

    @pl.when(z > 0)
    def _():
        go_dn(z).start()

    go_y(z).start()
    go_core(z, y).start()
    adj_swap = remote(adj_ref.at[:, 1 - c], adj_p, adjp_s, adjp_r, core_peer)

    idx[:rows] = jnp.transpose(jnp.broadcast_to(pos_ref[...], (128, rows)))
    idx[rows:] = jnp.transpose(jnp.broadcast_to(neg_ref[...], (128, rows)))
    acc[...] = jnp.zeros_like(acc)
    adj_load.wait()
    adj_swap.start()

    def use(s):
        block = feats[s]
        acc[:rows] += jnp.dot(adj[s // 2, s % 2], block, preferred_element_type=F32)
        lane = lax.broadcasted_iota(jnp.int32, (2 * rows, 128), 1) + s * rows
        parts = [
            jnp.where(idx[...] == lane + o, 1.0, 0.0).astype(BF16) for o in range(0, rows, 128)
        ]
        acc[rows:] += jnp.dot(
            jnp.concatenate(parts, axis=1), block, preferred_element_type=F32
        )

    use(me)

    def at(d, sign):
        zs = z + sign * d
        ok = (zs >= 0) & (zs < Z) & (d >= 0)
        return zs, (ok & (d > 0)) if sign > 0 else ok

    def gather_step(k, carry):
        zs, ok = at(k, -1)

        @pl.when(ok)
        def _():
            arrived(dev(zs, y, c))

            @pl.when(z < Z - 1)
            def _():
                go_up(zs).start()

            go_y(zs).start()
            go_core(zs, y).start()

        zt, okt = at(k, 1)

        @pl.when(okt)
        def _():
            arrived(dev(zt, y, c))

            @pl.when(z > 0)
            def _():
                go_dn(zt).start()

            go_y(zt).start()
            go_core(zt, y).start()

        for sign in (-1, 1):
            zy, oky = at(k - 1, sign)

            @pl.when(oky)
            def _():
                arrived(dev(zy, 1 - y, c))
                go_core(zy, 1 - y).start()

        def use_at(d, sign, yy, cc, wait):
            zu, oku = at(d, sign)

            @pl.when(oku)
            def _():
                s = dev(zu, yy, cc)
                if wait:
                    arrived(s)
                use(s)

        for sign in (-1, 1):
            use_at(k, sign, y, c, False)
            use_at(k - 1, sign, 1 - y, c, False)
            use_at(k - 1, sign, y, 1 - c, True)
            use_at(k - 2, sign, 1 - y, 1 - c, True)
        return carry

    lax.fori_loop(1, Z + 2, gather_step, 0)

    step = 64

    def rows_step(i, total):
        at_rows = pl.ds(pl.multiple_of(i * step, step), step)
        dg = jnp.concatenate([deg_ref[at_rows]] * (width // 128), axis=1)
        near = (acc[at_rows] / dg).astype(BF16)
        mean[at_rows] = near
        pre = jnp.dot(x_ref[at_rows], ws_ref[...], preferred_element_type=F32) + jnp.dot(
            near, wn_ref[...], preferred_element_type=F32
        )
        sig = jax.nn.sigmoid(pre)
        hid = pre * sig
        inv = 1.0 / jnp.sqrt(jnp.sum(hid * hid, axis=-1, keepdims=True) + 1e-05)
        emb = hid * inv
        pos = acc[pl.ds(pl.multiple_of(rows + i * step, step), step)]
        neg = acc[pl.ds(pl.multiple_of(2 * rows + i * step, step), step)]
        a = jnp.sum(emb * pos, axis=-1, keepdims=True)
        b = jnp.sum(emb * neg, axis=-1, keepdims=True)
        part = (
            jnp.maximum(-a, 0.0) + jnp.log1p(jnp.exp(-jnp.abs(a)))
            + jnp.maximum(b, 0.0) + jnp.log1p(jnp.exp(-jnp.abs(b)))
        )
        demb = -jax.nn.sigmoid(-a) * pos + jax.nn.sigmoid(b) * neg
        dhid = inv * (demb - emb * jnp.sum(demb * emb, axis=-1, keepdims=True))
        dp = (dhid * sig * (1.0 + pre * (1.0 - sig))).astype(BF16)
        dpre[at_rows] = dp
        gn32[at_rows] = (
            lax.dot_general(dp, wn_ref[...], (((1,), (1,)), ((), ())), preferred_element_type=F32)
            / dg
        )
        return total + jnp.sum(part, axis=0, keepdims=True)

    total = lax.fori_loop(0, rows // step, rows_step, jnp.zeros((1, 1), F32))
    gnt[0] = jnp.transpose(gn32[...]).astype(BF16)
    ex_gn = remote(gnt.at[0], gnt.at[1], ex_s.at[0], ex_r.at[0], core_peer)
    ex_gn.start()
    l_own[...] = jnp.broadcast_to(total, l_own.shape)
    ex_l = remote(l_own, l_core, ex_s.at[1], ex_r.at[1], core_peer)
    ex_l.start()

    scale = 1.0 / jnp.sqrt(F32(Z * 4 * rows))
    contract0 = (((0,), (0,)), ((), ()))
    gfull[0] = scale * lax.dot_general(x_ref[...], dpre[...], contract0, preferred_element_type=F32)
    gfull[1] = scale * lax.dot_general(mean[...], dpre[...], contract0, preferred_element_type=F32)
    ex_g = remote(gfull.at[1 - c], g_in, ex_s.at[2], ex_r.at[2], core_peer)
    ex_g.start()

    adj_swap.wait_recv()
    ex_gn.wait_recv()
    low = (z * 2) // Z

    def dest(j):
        return low * j + (1 - low) * (Z - 1 - j)

    def spread(zd, yd):
        return jnp.dot(gnt[0], adj[zd * 2 + yd, c], preferred_element_type=F32) + jnp.dot(
            gnt[1], adj_p[zd * 2 + yd], preferred_element_type=F32
        )

    def y_copy(zd):
        return remote(y_out.at[zd], y_in.at[zd], ys_s.at[zd], ys_r.at[zd], y_peer)

    def y_step(j, carry):
        zd = dest(j)
        y_out[zd] = spread(zd, 1 - y).astype(BF16)
        y_copy(zd).start()
        return carry

    lax.fori_loop(0, Z // 2, y_step, 0)

    ex_l.wait_recv()
    l_sum[...] = l_own[...] + l_core[...]
    ex_ly = remote(l_sum, l_y, ex_s.at[3], ex_r.at[3], y_peer)
    ex_ly.start()
    ex_g.wait_recv()
    other = pl.ds(pl.multiple_of((1 - y) * half, half), half)
    own = pl.ds(pl.multiple_of(y * half, half), half)
    gy_out[...] = (gfull[c, other] + g_in[other]).astype(BF16)
    ex_gy = remote(gy_out, gy_in, ex_s.at[4], ex_r.at[4], y_peer)
    ex_gy.start()

    lax.fori_loop(Z // 2, Z, y_step, 0)

    def up_copy(zd):
        return remote(z_out.at[zd], up_in.at[zd], zs_s.at[zd], up_r.at[zd], up_peer)

    def dn_copy(zd):
        return remote(z_out.at[zd], dn_in.at[zd], zs_s.at[zd], dn_r.at[zd], dn_peer)

    def z_step(j, carry):
        zd = dest(j)
        mine = spread(zd, y)
        y_copy(zd).wait_recv()
        gn32[...] = mine + y_in[zd].astype(F32)

        @pl.when(zd > z)
        def _():
            @pl.when(z > 0)
            def _():
                up_copy(zd).wait_recv()
                gn32[...] += up_in[zd].astype(F32)

            z_out[zd] = gn32[...].astype(BF16)
            up_copy(zd).start()

        @pl.when(zd < z)
        def _():
            @pl.when(z < Z - 1)
            def _():
                dn_copy(zd).wait_recv()
                gn32[...] += dn_in[zd].astype(F32)

            z_out[zd] = gn32[...].astype(BF16)
            dn_copy(zd).start()

        @pl.when(zd == z)
        def _():
            acc[:rows] = gn32[...]

        return carry

    lax.fori_loop(0, 1, z_step, 0)

    ex_ly.wait_recv()
    ex_gy.wait_recv()
    lz[z] = l_sum[...] + l_y[...]
    gz[z] = (gfull[c, own] + g_in[own] + gy_in[...].astype(F32)).astype(BF16)

    def gz_copy(k, slot):
        return remote(gz.at[slot], gz.at[slot], gz_s.at[k], gz_r.at[slot], dev((z + k) % Z, y, c))

    def lz_copy(k, slot):
        return remote(lz.at[slot], lz.at[slot], lz_s.at[k], lz_r.at[slot], dev((z + k) % Z, y, c))

    def gz_start(k, carry):
        gz_copy(k, z).start()
        lz_copy(k, z).start()
        return carry

    lax.fori_loop(1, Z, gz_start, 0)

    lax.fori_loop(1, Z, z_step, 0)

    def gz_wait(k, carry):
        slot = (z + k) % Z
        gz_copy(k, slot).wait_recv()
        lz_copy(k, slot).wait_recv()
        return carry

    lax.fori_loop(1, Z, gz_wait, 0)
    g_total, l_total = gz[0].astype(F32), lz[0]
    for k in range(1, Z):
        g_total = g_total + gz[k].astype(F32)
        l_total = l_total + lz[k]
    gh[y] = g_total.astype(BF16)
    ex_gh = remote(gh.at[y], gh.at[y], ex_s.at[5], ex_r.at[5], y_peer)
    ex_gh.start()
    loss_ref[...] = l_total / F32(Z * 4 * rows)

    direct = lax.dot_general(
        dpre[...], ws_ref[...], (((1,), (1,)), ((), ())), preferred_element_type=F32
    )

    @pl.when(z > 0)
    def _():
        up_copy(z).wait_recv()
        acc[:rows] += up_in[z].astype(F32)

    @pl.when(z < Z - 1)
    def _():
        dn_copy(z).wait_recv()
        acc[:rows] += dn_in[z].astype(F32)

    remote(gh.at[1 - y], gh.at[1 - y], ex_s.at[5], ex_r.at[5], y_peer).wait_recv()
    ex_gp = remote(gh, gp, ex_s.at[6], ex_r.at[6], core_peer)
    ex_gp.start()
    gfeat_ref[...] = direct + jnp.transpose(acc[:rows])
    ex_gp.wait_recv()

    @pl.when(c == 0)
    def _():
        for h in range(2):
            gself_ref[h * half : (h + 1) * half] = gh[h].astype(F32)
            gneigh_ref[h * half : (h + 1) * half] = gp[h].astype(F32)

    @pl.when(c == 1)
    def _():
        for h in range(2):
            gself_ref[h * half : (h + 1) * half] = gp[h].astype(F32)
            gneigh_ref[h * half : (h + 1) * half] = gh[h].astype(F32)

    def sent(zs, carry):
        @pl.when((zs <= z) & (z < Z - 1))
        def _():
            go_up(zs).wait_send()

        @pl.when((zs >= z) & (z > 0))
        def _():
            go_dn(zs).wait_send()

        go_y(zs).wait_send()
        go_core(zs, 0).wait_send()
        go_core(zs, 1).wait_send()
        y_copy(zs).wait_send()

        @pl.when(zs != z)
        def _():
            up_copy(zs).wait_send()

        return carry

    lax.fori_loop(0, Z, sent, 0)

    def sent_z(k, carry):
        gz_copy(k, z).wait_send()
        lz_copy(k, z).wait_send()
        return carry

    lax.fori_loop(1, Z, sent_z, 0)
    for copy in (adj_swap, ex_gn, ex_l, ex_g, ex_ly, ex_gy, ex_gh, ex_gp):
        copy.wait_send()


def on_device(
    features, self_weight, neigh_weight, tile_vals, tile_cols, tile_count, pos_index, neg_index
):
    rows, width = features.shape
    shards = lax.axis_size("row")
    Z = shards // 4
    adj, degree = dense_rows(tile_vals, tile_cols, tile_count, shards)
    adj = adj.reshape(shards // 2, 2, rows, rows)
    vmem = pl.BlockSpec(memory_space=pltpu.VMEM)
    half = rows // 2
    dma = pltpu.SemaphoreType.DMA
    loss, grad_self, grad_neigh, grad_feat = pl.pallas_call(
        functools.partial(layer_kernel, Z),
        in_specs=[vmem, vmem, vmem, pl.BlockSpec(memory_space=pl.ANY), vmem, vmem, vmem],
        out_specs=[vmem] * 4,
        out_shape=[
            jax.ShapeDtypeStruct((8, 128), F32),
            jax.ShapeDtypeStruct((width, width), F32),
            jax.ShapeDtypeStruct((width, width), F32),
            jax.ShapeDtypeStruct((rows, width), F32),
        ],
        scratch_shapes=[
            pltpu.VMEM((shards, rows, width), BF16),
            pltpu.VMEM((shards // 2, 2, rows, rows), BF16),
            pltpu.VMEM((shards // 2, rows, rows), BF16),
            pltpu.VMEM((2 * rows, 128), jnp.int32),
            pltpu.VMEM((3 * rows, width), F32),
            pltpu.VMEM((rows, width), BF16),
            pltpu.VMEM((rows, width), BF16),
            pltpu.VMEM((2, width, rows), BF16),
            pltpu.VMEM((rows, width), F32),
            pltpu.VMEM((2, width, width), F32),
            pltpu.VMEM((width, width), F32),
            pltpu.VMEM((half, width), BF16),
            pltpu.VMEM((half, width), BF16),
            pltpu.VMEM((Z, half, width), BF16),
            pltpu.VMEM((2, half, width), BF16),
            pltpu.VMEM((2, half, width), BF16),
            pltpu.VMEM((8, 128), F32),
            pltpu.VMEM((8, 128), F32),
            pltpu.VMEM((8, 128), F32),
            pltpu.VMEM((8, 128), F32),
            pltpu.VMEM((Z, 8, 128), F32),
            pltpu.VMEM((Z, width, rows), BF16),
            pltpu.VMEM((Z, width, rows), BF16),
            pltpu.VMEM((Z, width, rows), BF16),
            pltpu.VMEM((Z, width, rows), BF16),
            pltpu.VMEM((Z, width, rows), BF16),
            dma(()), dma(()), dma(()), dma((shards,)), dma((Z,)), dma((Z,)), dma((Z,)),
            dma((2 * Z,)), dma((7,)), dma((7,)), dma((Z,)), dma((Z,)), dma((Z,)), dma((Z,)),
            dma((Z,)), dma((Z,)), dma((Z,)), dma((Z,)), dma((Z,)),
        ],
        compiler_params=pltpu.CompilerParams(
            collective_id=0, has_side_effects=True, vmem_limit_bytes=56 * 1024 * 1024
        ),
    )(
        features, self_weight, neigh_weight, adj, degree,
        pos_index.reshape(1, rows), neg_index.reshape(1, rows),
    )
    return (loss[0, :1], grad_self, grad_neigh, grad_feat)


def solution(mesh):
    placed = (
        P(("groups", "row"), None),
        P(),
        P(),
        P(("groups", "row"), None, None, None),
        P(("groups", "row"), None),
        P(("groups", "row")),
        P(("groups", "row")),
        P(("groups", "row")),
    )
    return jax.shard_map(
        on_device,
        mesh=mesh,
        in_specs=placed,
        out_specs=(P("groups"), P("groups", None), P("groups", None), P(("groups", "row"), None)),
        check_vma=False,
    )
```

time: 252 us -> 70.3 us (0.28)
  waiting for transfers between devices: 118 us -> 0 us
  Pallas kernels: 0 us -> 59.4 us
  other arithmetic: 45 us -> 0 us
  blocking collectives: 32.3 us -> 0 us
  matrix products: 22.9 us -> 0 us
  between operations: 15.6 us -> 0.67 us
  local copies, waits for them, and re-layouts: 17.4 us -> 9.5 us
    reduce_scatter x1 -> x0, waiting for transfers between devices: 74.9 us -> none  [on_device(): lax.psum_scatter(flat_total, 'row', scatter_dimension=0, tiled=True)]
    pallas_call x0 -> x2, Pallas kernels: none -> 59.4 us  [the longest x1 54.3 us: on_device(): pl.pallas_call(functools.partial(layer_kernel, Z), in_specs=[vmem, vmem,...]
    all_gather x1 -> x0, waiting for transfers between devices: 38.2 us -> none  [on_device(): all_nodes = lax.all_gather(features, 'row', axis=0, tiled=True)]
    scatter-add x1 -> x0, other arithmetic: 37.9 us -> none  [on_device(): column_total = jnp.zeros((column_tiles, tile_size, width_f), jnp.float32)...]
    psum x1 -> x0, blocking collectives: 32.3 us -> none  [on_device(): lax.psum((self_part, neigh_part, loss_part), 'row')]
    dot_general x8 -> x0, matrix products: 22.9 us -> none  [the longest x1 11.4 us: on_device(): jnp.einsum('rsij,rif->rsjf', masked, g_blocks, preferred_element_type=jnp...]
    gather x5 -> x0, local copies, waits for them, and re-layouts: 10.7 us -> none  [the longest x1 8.15 us: on_device(): picked = node_blocks[tile_cols]]
    unnamed x10 -> x11, local copies, waits for them, and re-layouts: 3.48 us -> 8.32 us
  transfers between devices with their start and end apart: 3 -> 0, of which waited for: 3 -> 0; matrix products, arithmetic and copies ran while one was open for 24% -> 0% of each run, Pallas kernels for 0% -> 0%
where the time goes in v1:
time: 70.3 us; the launch traced here: 69.6 us
  Pallas kernels  59.4 us (84%)
  local copies, waits for them, and re-layouts  9.5 us (14%)
    pallas_call x1, Pallas kernels, on_device(): pl.pallas_call(functools.partial(layer_kernel, Z), in_specs=[vmem, vmem,...  54.3 us
    unnamed x11, local copies, waits for them, and re-layouts  8.32 us
    pallas_call x1, Pallas kernels, dense_rows(): pl.pallas_call(dense_kernel, grid_spec=pltpu.PrefetchScalarGridSpec(num_s...  5.07 us

profile of v1, /device:TPU:0, one launch (start us, length us, event | category | flops | bytes accessed | tf_op | source)
XLA Modules:
  0.0 69.6 jit_solution(10585100580484618036)
XLA Ops:
  0.6 0.0 copy-start.2
  0.6 0.7 copy-done.2
  1.3 0.0 copy-start.3
  1.3 0.7 copy-done.3
  2.0 5.1 %shard_map.111 = (bf16[16,256,256]{2,1,0:T(8,128)(2,1)S(1)}, f32[256,128]{1,0:T(8,128)S(1)}) custom-call(s32[2,64]{1,0:T(2,128)S(1)} %copy-done.2, s32[2]{0:T(128)S(1)} %copy-done.3, bf16[2,64,128,128]{3,2,1,0:T(8,128)(2,1)} %tiles_ref.1), custom_call_target="tpu_custom_call" | custom-call | tf_op jit(solution)/shard_map/pallas_call | solution.py:57
  7.0 0.0 copy-start
  7.1 1.3 %copy-done = bf16[16,256,256]{2,1,0:T(8,128)(2,1)} copy-done((bf16[16,256,256]{2,1,0:T(8,128)(2,1)}, bf16[16,256,256]{2,1,0:T(8,128)(2,1)S(1)}, u32[]{:S(2)}) %copy-start) | copy-done | bytes 2097176
  8.4 0.0 copy-start.1
  8.4 0.7 copy-done.1
  9.0 54.3 %shard_map.112 = (f32[8,128]{1,0:T(8,128)}, f32[256,256]{1,0:T(8,128)}, f32[256,256]{1,0:T(8,128)}, f32[256,256]{1,0:T(8,128)}) custom-call(bf16[256,256]{1,0:T(8,128)(2,1)} %x_ref.1, bf16[256,256]{1,0:T(8,128)(2,1)} %ws_ref.1, bf16[256,256]{1,0:T(8,128)(2,1)} %wn_ref.1, bf16[8,2,256,256]{3,2,1,0:T(8,128)(2,1)} %bitcast.4, f32[256,128]{1,0:T(8,128)} %copy-done.1, ...), custom_call_target="tpu_custom_call" | custom-call | tf_op jit(solution)/shard_map/pallas_call | solution.py:461
  63.4 1.2 %slice.3 = f32[1,1]{1,0:T(1,128)} slice(f32[8,128]{1,0:T(8,128)} %get-tuple-element.12), slice={[0:1], [0:1]} | slice | bytes 8 | tf_op jit(solution)/shard_map/slice | solution.py:509
  64.6 1.7 %copy.15 = f32[256,256]{1,0:T(8,128)} copy(f32[256,256]{1,0:T(8,128)} %get-tuple-element.21) | data formatting | bytes 524288
  66.2 1.7 %copy.16 = f32[256,256]{1,0:T(8,128)} copy(f32[256,256]{1,0:T(8,128)} %get-tuple-element.22) | data formatting | bytes 524288
  67.9 1.7 %copy.17 = f32[256,256]{1,0:T(8,128)} copy(f32[256,256]{1,0:T(8,128)} %get-tuple-element.23) | data formatting | bytes 524288
Async XLA Ops:
  0.6 0.7 copy-start.2
  1.3 0.7 copy-start.3
  7.0 1.3 %copy-start = (bf16[16,256,256]{2,1,0:T(8,128)(2,1)}, bf16[16,256,256]{2,1,0:T(8,128)(2,1)S(1)}, u32[]{:S(2)}) copy-start(bf16[16,256,256]{2,1,0:T(8,128)(2,1)S(1)} %get-tuple-element.10) | copy-start | bytes 6291460
  8.4 0.7 copy-start.1

commit v2 on v1

--- a/solution.py
+++ b/solution.py
@@ -70,21 +70,23 @@
             jax.ShapeDtypeStruct((shards, tile_rows * tile, 2 * tile), BF16),
             jax.ShapeDtypeStruct((tile_rows * tile, tile), F32),
         ],
-        compiler_params=pltpu.CompilerParams(vmem_limit_bytes=48 * 1024 * 1024),
+        compiler_params=pltpu.CompilerParams(
+            vmem_limit_bytes=48 * 1024 * 1024
+        ),
     )(tile_cols, tile_count, tile_vals)
 
 
 def layer_kernel(
-    Z, x_ref, ws_ref, wn_ref, adj_ref, deg_ref, pos_ref, neg_ref,
-    loss_ref, gself_ref, gneigh_ref, gfeat_ref,
-    feats, adj, adj_p, idx, acc, dpre, mean,
+    Z, x_hbm, ws_hbm, wn_hbm, adj, deg_hbm, pos_ref, neg_ref,
+    loss_ref, grads_ref, gfeat_ref,
+    feats, ws, wn, deg, adj_p, idx, acc, dpre, mean,
     gnt, gn32, gfull, g_in, gy_out, gy_in, gz, gh, gp,
     l_own, l_core, l_sum, l_y, lz,
-    y_out, y_in, z_out, up_in, dn_in,
-    adj_sem, adjp_s, adjp_r, recv, up_s, dn_s, y_s, core_s,
+    y_out, y_in, z_out, up_in, dn_in, tsum, town,
+    load_sem, adjp_s, adjp_r, recv, up_s, dn_s, y_s, core_s,
     ex_s, ex_r, gz_s, gz_r, lz_s, lz_r, ys_s, ys_r, zs_s, up_r, dn_r,
 ):
-    rows, width = x_ref.shape
+    rows, width = x_hbm.shape
     half = rows // 2
     me = lax.axis_index("row")
     z, y, c = me // 4, (me // 2) % 2, me % 2
@@ -102,8 +104,15 @@
             device_id={"row": target}, device_id_type=MESH,
         )
 
-    adj_load = pltpu.make_async_copy(adj_ref, adj, adj_sem)
-    adj_load.start()
+    loads = [
+        pltpu.make_async_copy(x_hbm, feats.at[me], load_sem.at[0]),
+        pltpu.make_async_copy(ws_hbm, ws, load_sem.at[1]),
+        pltpu.make_async_copy(wn_hbm, wn, load_sem.at[2]),
+        pltpu.make_async_copy(deg_hbm, deg, load_sem.at[3]),
+    ]
+    loads[0].start()
+    for load in loads[1:]:
+        load.start()
 
     barrier = pltpu.get_barrier_semaphore()
     pl.semaphore_signal(barrier, inc=1, device_id={"row": core_peer}, device_id_type=MESH)
@@ -112,44 +121,47 @@
         pl.semaphore_signal(
             barrier, inc=1, device_id={"row": dev((z + k) % Z, y, c)}, device_id_type=MESH
         )
-    feats[me] = x_ref[...]
+    loads[0].wait()
     pl.semaphore_wait(barrier, Z + 1)
 
-    def go_up(zs):
-        s = dev(zs, y, c)
-        return remote(feats.at[s], feats.at[s], up_s.at[zs], recv.at[s], up_peer)
-
-    def go_dn(zs):
-        s = dev(zs, y, c)
-        return remote(feats.at[s], feats.at[s], dn_s.at[zs], recv.at[s], dn_peer)
-
-    def go_y(zs):
-        s = dev(zs, y, c)
-        return remote(feats.at[s], feats.at[s], y_s.at[zs], recv.at[s], y_peer)
-
-    def go_core(zs, yy):
-        s = dev(zs, yy, c)
-        return remote(feats.at[s], feats.at[s], core_s.at[zs * 2 + yy], recv.at[s], core_peer)
-
-    def arrived(s):
-        remote(feats.at[s], feats.at[s], core_s.at[0], recv.at[s], core_peer).wait_recv()
-
-    @pl.when(z < Z - 1)
-    def _():
-        go_up(z).start()
-
-    @pl.when(z > 0)
-    def _():
-        go_dn(z).start()
-
-    go_y(z).start()
-    go_core(z, y).start()
-    adj_swap = remote(adj_ref.at[:, 1 - c], adj_p, adjp_s, adjp_r, core_peer)
+    def part(s, h):
+        return feats.at[s, pl.ds(h * half, half)]
+
+    def hop(s, h, sem, target):
+        return remote(part(s, h), part(s, h), sem, recv.at[2 * s + h], target)
+
+    def go_up(zs, h):
+        return hop(dev(zs, y, c), h, up_s.at[2 * zs + h], up_peer)
+
+    def go_dn(zs, h):
+        return hop(dev(zs, y, c), h, dn_s.at[2 * zs + h], dn_peer)
+
+    def go_y(zs, h):
+        return hop(dev(zs, y, c), h, y_s.at[2 * zs + h], y_peer)
+
+    def go_core(zs, yy, h):
+        return hop(dev(zs, yy, c), h, core_s.at[4 * zs + 2 * yy + h], core_peer)
+
+    def arrived(s, h):
+        hop(s, h, core_s.at[0], core_peer).wait_recv()
+
+    for h in range(2):
+        @pl.when(z < Z - 1)
+        def _():
+            go_up(z, h).start()
+
+        @pl.when(z > 0)
+        def _():
+            go_dn(z, h).start()
+
+        go_y(z, h).start()
+        go_core(z, y, h).start()
+
+    adj_swap = remote(adj.at[:, 1 - c], adj_p, adjp_s, adjp_r, core_peer)
 
     idx[:rows] = jnp.transpose(jnp.broadcast_to(pos_ref[...], (128, rows)))
     idx[rows:] = jnp.transpose(jnp.broadcast_to(neg_ref[...], (128, rows)))
     acc[...] = jnp.zeros_like(acc)
-    adj_load.wait()
     adj_swap.start()
 
     def use(s):
@@ -171,39 +183,41 @@
         return zs, (ok & (d > 0)) if sign > 0 else ok
 
     def gather_step(k, carry):
-        zs, ok = at(k, -1)
-
-        @pl.when(ok)
-        def _():
-            arrived(dev(zs, y, c))
-
-            @pl.when(z < Z - 1)
-            def _():
-                go_up(zs).start()
-
-            go_y(zs).start()
-            go_core(zs, y).start()
-
-        zt, okt = at(k, 1)
-
-        @pl.when(okt)
-        def _():
-            arrived(dev(zt, y, c))
-
-            @pl.when(z > 0)
-            def _():
-                go_dn(zt).start()
-
-            go_y(zt).start()
-            go_core(zt, y).start()
-
-        for sign in (-1, 1):
-            zy, oky = at(k - 1, sign)
-
-            @pl.when(oky)
-            def _():
-                arrived(dev(zy, 1 - y, c))
-                go_core(zy, 1 - y).start()
+        for h in range(2):
+            zs, ok = at(k, -1)
+
+            @pl.when(ok)
+            def _():
+                arrived(dev(zs, y, c), h)
+
+                @pl.when(z < Z - 1)
+                def _():
+                    go_up(zs, h).start()
+
+                go_y(zs, h).start()
+                go_core(zs, y, h).start()
+
+            zt, okt = at(k, 1)
+
+            @pl.when(okt)
+            def _():
+                arrived(dev(zt, y, c), h)
+
+                @pl.when(z > 0)
+                def _():
+                    go_dn(zt, h).start()
+
+                go_y(zt, h).start()
+                go_core(zt, y, h).start()
+
+        for h in range(2):
+            for sign in (-1, 1):
+                zy, oky = at(k - 1, sign)
+
+                @pl.when(oky)
+                def _():
+                    arrived(dev(zy, 1 - y, c), h)
+                    go_core(zy, 1 - y, h).start()
 
         def use_at(d, sign, yy, cc, wait):
             zu, oku = at(d, sign)
@@ -212,7 +226,8 @@
             def _():
                 s = dev(zu, yy, cc)
                 if wait:
-                    arrived(s)
+                    arrived(s, 0)
+                    arrived(s, 1)
                 use(s)
 
         for sign in (-1, 1):
@@ -225,14 +240,16 @@
     lax.fori_loop(1, Z + 2, gather_step, 0)
 
     step = 64
+    for load in loads[1:]:
+        load.wait()
 
     def rows_step(i, total):
         at_rows = pl.ds(pl.multiple_of(i * step, step), step)
-        dg = jnp.concatenate([deg_ref[at_rows]] * (width // 128), axis=1)
+        dg = jnp.concatenate([deg[at_rows]] * (width // 128), axis=1)
         near = (acc[at_rows] / dg).astype(BF16)
         mean[at_rows] = near
-        pre = jnp.dot(x_ref[at_rows], ws_ref[...], preferred_element_type=F32) + jnp.dot(
-            near, wn_ref[...], preferred_element_type=F32
+        pre = jnp.dot(feats[me, at_rows], ws[...], preferred_element_type=F32) + jnp.dot(
+            near, wn[...], preferred_element_type=F32
         )
         sig = jax.nn.sigmoid(pre)
         hid = pre * sig
@@ -251,12 +268,12 @@
         dp = (dhid * sig * (1.0 + pre * (1.0 - sig))).astype(BF16)
         dpre[at_rows] = dp
         gn32[at_rows] = (
-            lax.dot_general(dp, wn_ref[...], (((1,), (1,)), ((), ())), preferred_element_type=F32)
+            lax.dot_general(dp, wn[...], (((1,), (1,)), ((), ())), preferred_element_type=F32)
             / dg
         )
         return total + jnp.sum(part, axis=0, keepdims=True)
 
-    total = lax.fori_loop(0, rows // step, rows_step, jnp.zeros((1, 1), F32))
+    total = lax.fori_loop(0, rows // step, rows_step, jnp.zeros((1, 1), F32), unroll=True)
     gnt[0] = jnp.transpose(gn32[...]).astype(BF16)
     ex_gn = remote(gnt.at[0], gnt.at[1], ex_s.at[0], ex_r.at[0], core_peer)
     ex_gn.start()
@@ -266,7 +283,7 @@
 
     scale = 1.0 / jnp.sqrt(F32(Z * 4 * rows))
     contract0 = (((0,), (0,)), ((), ()))
-    gfull[0] = scale * lax.dot_general(x_ref[...], dpre[...], contract0, preferred_element_type=F32)
+    gfull[0] = scale * lax.dot_general(feats[me], dpre[...], contract0, preferred_element_type=F32)
     gfull[1] = scale * lax.dot_general(mean[...], dpre[...], contract0, preferred_element_type=F32)
     ex_g = remote(gfull.at[1 - c], g_in, ex_s.at[2], ex_r.at[2], core_peer)
     ex_g.start()
@@ -276,23 +293,27 @@
     low = (z * 2) // Z
 
     def dest(j):
-        return low * j + (1 - low) * (Z - 1 - j)
-
-    def spread(zd, yd):
-        return jnp.dot(gnt[0], adj[zd * 2 + yd, c], preferred_element_type=F32) + jnp.dot(
-            gnt[1], adj_p[zd * 2 + yd], preferred_element_type=F32
-        )
-
-    def y_copy(zd):
-        return remote(y_out.at[zd], y_in.at[zd], ys_s.at[zd], ys_r.at[zd], y_peer)
-
-    def y_step(j, carry):
-        zd = dest(j)
-        y_out[zd] = spread(zd, 1 - y).astype(BF16)
-        y_copy(zd).start()
-        return carry
-
-    lax.fori_loop(0, Z // 2, y_step, 0)
+        own_at = low * z + (1 - low) * (Z - 1 - z)
+        skip, last = (j + Z - own_at) // Z, (j + 1) // Z
+        return last * z + (1 - last) * (low * (j + skip) + (1 - low) * (Z - 1 - j - skip))
+
+    def spread(zd, h, yd):
+        at_half = pl.ds(pl.multiple_of(h * half, half), half)
+        return jnp.dot(
+            gnt[0, at_half], adj[zd * 2 + yd, c], preferred_element_type=F32
+        ) + jnp.dot(gnt[1, at_half], adj_p[zd * 2 + yd], preferred_element_type=F32)
+
+    def y_copy(i):
+        return remote(y_out.at[i], y_in.at[i], ys_s.at[i], ys_r.at[i], y_peer)
+
+    def y_step(i, carry):
+        zd, h = dest(i // 2), i % 2
+        slot = 2 * zd + h
+        y_out[slot] = spread(zd, h, 1 - y).astype(BF16)
+        y_copy(slot).start()
+        return carry
+
+    lax.fori_loop(0, 1, y_step, 0)
 
     ex_l.wait_recv()
     l_sum[...] = l_own[...] + l_core[...]
@@ -305,43 +326,44 @@
     ex_gy = remote(gy_out, gy_in, ex_s.at[4], ex_r.at[4], y_peer)
     ex_gy.start()
 
-    lax.fori_loop(Z // 2, Z, y_step, 0)
-
-    def up_copy(zd):
-        return remote(z_out.at[zd], up_in.at[zd], zs_s.at[zd], up_r.at[zd], up_peer)
-
-    def dn_copy(zd):
-        return remote(z_out.at[zd], dn_in.at[zd], zs_s.at[zd], dn_r.at[zd], dn_peer)
-
-    def z_step(j, carry):
-        zd = dest(j)
-        mine = spread(zd, y)
-        y_copy(zd).wait_recv()
-        gn32[...] = mine + y_in[zd].astype(F32)
+    lax.fori_loop(1, 2 * Z - 2, y_step, 0)
+
+    def up_copy(i):
+        return remote(z_out.at[i], up_in.at[i], zs_s.at[i], up_r.at[i], up_peer)
+
+    def dn_copy(i):
+        return remote(z_out.at[i], dn_in.at[i], zs_s.at[i], dn_r.at[i], dn_peer)
+
+    def z_step(i, carry):
+        zd, h = dest(i // 2), i % 2
+        slot = 2 * zd + h
+        mine = spread(zd, h, y)
+        y_copy(slot).wait_recv()
+        tsum[...] = mine + y_in[slot].astype(F32)
 
         @pl.when(zd > z)
         def _():
             @pl.when(z > 0)
             def _():
-                up_copy(zd).wait_recv()
-                gn32[...] += up_in[zd].astype(F32)
-
-            z_out[zd] = gn32[...].astype(BF16)
-            up_copy(zd).start()
+                up_copy(slot).wait_recv()
+                tsum[...] += up_in[slot].astype(F32)
+
+            z_out[slot] = tsum[...].astype(BF16)
+            up_copy(slot).start()
 
         @pl.when(zd < z)
         def _():
             @pl.when(z < Z - 1)
             def _():
-                dn_copy(zd).wait_recv()
-                gn32[...] += dn_in[zd].astype(F32)
-
-            z_out[zd] = gn32[...].astype(BF16)
-            dn_copy(zd).start()
+                dn_copy(slot).wait_recv()
+                tsum[...] += dn_in[slot].astype(F32)
+
+            z_out[slot] = tsum[...].astype(BF16)
+            dn_copy(slot).start()
 
         @pl.when(zd == z)
         def _():
-            acc[:rows] = gn32[...]
+            town[h] = tsum[...]
 
         return carry
 
@@ -383,55 +405,55 @@
     ex_gh.start()
     loss_ref[...] = l_total / F32(Z * 4 * rows)
 
-    direct = lax.dot_general(
-        dpre[...], ws_ref[...], (((1,), (1,)), ((), ())), preferred_element_type=F32
-    )
-
-    @pl.when(z > 0)
-    def _():
-        up_copy(z).wait_recv()
-        acc[:rows] += up_in[z].astype(F32)
-
-    @pl.when(z < Z - 1)
-    def _():
-        dn_copy(z).wait_recv()
-        acc[:rows] += dn_in[z].astype(F32)
+    lax.fori_loop(2 * Z - 2, 2 * Z, y_step, 0)
+    lax.fori_loop(Z, 2 * Z - 2, z_step, 0)
 
     remote(gh.at[1 - y], gh.at[1 - y], ex_s.at[5], ex_r.at[5], y_peer).wait_recv()
     ex_gp = remote(gh, gp, ex_s.at[6], ex_r.at[6], core_peer)
     ex_gp.start()
-    gfeat_ref[...] = direct + jnp.transpose(acc[:rows])
+
+    lax.fori_loop(2 * Z - 2, 2 * Z, z_step, 0)
+
+    gn32[...] = lax.dot_general(
+        dpre[...], ws[...], (((1,), (1,)), ((), ())), preferred_element_type=F32
+    )
     ex_gp.wait_recv()
-
-    @pl.when(c == 0)
-    def _():
+    for h in range(2):
+        grads_ref[c, h * half : (h + 1) * half] = gh[h]
+        grads_ref[1 - c, h * half : (h + 1) * half] = gp[h]
+
+    for h in range(2):
+        @pl.when(z > 0)
+        def _():
+            up_copy(2 * z + h).wait_recv()
+            town[h] += up_in[2 * z + h].astype(F32)
+
+        @pl.when(z < Z - 1)
+        def _():
+            dn_copy(2 * z + h).wait_recv()
+            town[h] += dn_in[2 * z + h].astype(F32)
+
+        at_half = slice(h * half, (h + 1) * half)
+        gfeat_ref[:, at_half] = gn32[:, at_half] + jnp.transpose(town[h])
+
+    def sent(zs, carry):
         for h in range(2):
-            gself_ref[h * half : (h + 1) * half] = gh[h].astype(F32)
-            gneigh_ref[h * half : (h + 1) * half] = gp[h].astype(F32)
-
-    @pl.when(c == 1)
-    def _():
-        for h in range(2):
-            gself_ref[h * half : (h + 1) * half] = gp[h].astype(F32)
-            gneigh_ref[h * half : (h + 1) * half] = gh[h].astype(F32)
-
-    def sent(zs, carry):
-        @pl.when((zs <= z) & (z < Z - 1))
-        def _():
-            go_up(zs).wait_send()
-
-        @pl.when((zs >= z) & (z > 0))
-        def _():
-            go_dn(zs).wait_send()
-
-        go_y(zs).wait_send()
-        go_core(zs, 0).wait_send()
-        go_core(zs, 1).wait_send()
-        y_copy(zs).wait_send()
-
-        @pl.when(zs != z)
-        def _():
-            up_copy(zs).wait_send()
+            @pl.when((zs <= z) & (z < Z - 1))
+            def _():
+                go_up(zs, h).wait_send()
+
+            @pl.when((zs >= z) & (z > 0))
+            def _():
+                go_dn(zs, h).wait_send()
+
+            go_y(zs, h).wait_send()
+            go_core(zs, 0, h).wait_send()
+            go_core(zs, 1, h).wait_send()
+            y_copy(2 * zs + h).wait_send()
+
+            @pl.when(zs != z)
+            def _():
+                up_copy(2 * zs + h).wait_send()
 
         return carry
 
@@ -445,6 +467,13 @@
     lax.fori_loop(1, Z, sent_z, 0)
     for copy in (adj_swap, ex_gn, ex_l, ex_g, ex_ly, ex_gy, ex_gh, ex_gp):
         copy.wait_send()
+
+
+def finish_kernel(loss_ref, grads_ref, gfeat_ref, loss_out, gself_out, gneigh_out, gfeat_out):
+    loss_out[0] = loss_ref[0, 0]
+    gself_out[...] = grads_ref[0].astype(F32)
+    gneigh_out[...] = grads_ref[1].astype(F32)
+    gfeat_out[...] = gfeat_ref[...]
 
 
 def on_device(
@@ -456,21 +485,23 @@
     adj, degree = dense_rows(tile_vals, tile_cols, tile_count, shards)
     adj = adj.reshape(shards // 2, 2, rows, rows)
     vmem = pl.BlockSpec(memory_space=pltpu.VMEM)
+    anywhere = pl.BlockSpec(memory_space=pl.ANY)
     half = rows // 2
     dma = pltpu.SemaphoreType.DMA
-    loss, grad_self, grad_neigh, grad_feat = pl.pallas_call(
+    parts = pl.pallas_call(
         functools.partial(layer_kernel, Z),
-        in_specs=[vmem, vmem, vmem, pl.BlockSpec(memory_space=pl.ANY), vmem, vmem, vmem],
-        out_specs=[vmem] * 4,
+        in_specs=[anywhere] * 3 + [vmem, anywhere, vmem, vmem],
+        out_specs=[vmem] * 3,
         out_shape=[
             jax.ShapeDtypeStruct((8, 128), F32),
-            jax.ShapeDtypeStruct((width, width), F32),
-            jax.ShapeDtypeStruct((width, width), F32),
+            jax.ShapeDtypeStruct((2, width, width), BF16),
             jax.ShapeDtypeStruct((rows, width), F32),
         ],
         scratch_shapes=[
             pltpu.VMEM((shards, rows, width), BF16),
-            pltpu.VMEM((shards // 2, 2, rows, rows), BF16),
+            pltpu.VMEM((width, width), BF16),
+            pltpu.VMEM((width, width), BF16),
+            pltpu.VMEM((rows, 128), F32),
             pltpu.VMEM((shards // 2, rows, rows), BF16),
             pltpu.VMEM((2 * rows, 128), jnp.int32),
             pltpu.VMEM((3 * rows, width), F32),
@@ -490,23 +521,35 @@
             pltpu.VMEM((8, 128), F32),
             pltpu.VMEM((8, 128), F32),
             pltpu.VMEM((Z, 8, 128), F32),
-            pltpu.VMEM((Z, width, rows), BF16),
-            pltpu.VMEM((Z, width, rows), BF16),
-            pltpu.VMEM((Z, width, rows), BF16),
-            pltpu.VMEM((Z, width, rows), BF16),
-            pltpu.VMEM((Z, width, rows), BF16),
-            dma(()), dma(()), dma(()), dma((shards,)), dma((Z,)), dma((Z,)), dma((Z,)),
-            dma((2 * Z,)), dma((7,)), dma((7,)), dma((Z,)), dma((Z,)), dma((Z,)), dma((Z,)),
-            dma((Z,)), dma((Z,)), dma((Z,)), dma((Z,)), dma((Z,)),
+            pltpu.VMEM((2 * Z, half, rows), BF16),
+            pltpu.VMEM((2 * Z, half, rows), BF16),
+            pltpu.VMEM((2 * Z, half, rows), BF16),
+            pltpu.VMEM((2 * Z, half, rows), BF16),
+            pltpu.VMEM((2 * Z, half, rows), BF16),
+            pltpu.VMEM((half, rows), F32),
+            pltpu.VMEM((2, half, rows), F32),
+            dma((4,)), dma(()), dma(()), dma((2 * shards,)), dma((2 * Z,)), dma((2 * Z,)),
+            dma((2 * Z,)), dma((4 * Z,)), dma((7,)), dma((7,)), dma((Z,)), dma((Z,)), dma((Z,)),
+            dma((Z,)), dma((2 * Z,)), dma((2 * Z,)), dma((2 * Z,)), dma((2 * Z,)), dma((2 * Z,)),
         ],
         compiler_params=pltpu.CompilerParams(
-            collective_id=0, has_side_effects=True, vmem_limit_bytes=56 * 1024 * 1024
+            collective_id=0, has_side_effects=True,
+            vmem_limit_bytes=8 * 1024 * 1024 + shards * rows * rows * 2 * 5,
         ),
     )(
         features, self_weight, neigh_weight, adj, degree,
         pos_index.reshape(1, rows), neg_index.reshape(1, rows),
     )
-    return (loss[0, :1], grad_self, grad_neigh, grad_feat)
+    square = jax.ShapeDtypeStruct((width, width), F32)
+    return pl.pallas_call(
+        finish_kernel,
+        in_specs=[vmem] * 3,
+        out_specs=[pl.BlockSpec(memory_space=pltpu.SMEM)] + [vmem] * 3,
+        out_shape=[
+            jax.ShapeDtypeStruct((1,), F32), square, square,
+            jax.ShapeDtypeStruct((rows, width), F32),
+        ],
+    )(*parts)
 
 
 def solution(mesh):

time: 70.3 us -> 57.3 us (0.82)
  Pallas kernels: 59.4 us -> 52.4 us
  local copies, waits for them, and re-layouts: 9.5 us -> 3.38 us
    pallas_call x1 -> x2, Pallas kernels: 54.3 us -> 48.4 us  [the longest x1 46.5 us: on_device(): pl.pallas_call(functools.partial(layer_kernel, Z), in_specs=[anywhere] *...]
    unnamed x11 -> x20, local copies, waits for them, and re-layouts: 8.32 us -> 3.38 us
    slice x1 -> x0, local copies, waits for them, and re-layouts: 1.19 us -> none  [on_device(): return (loss[0, :1], grad_self, grad_neigh, grad_feat)]
    pallas_call x1, Pallas kernels: 5.07 us -> 3.97 us  [dense_rows(): pl.pallas_call(dense_kernel, grid_spec=pltpu.PrefetchScalarGridSpec(num_s...]
where the time goes in v2:
time: 57.3 us; the launch traced here: 56.5 us
  Pallas kernels  52.4 us (91%)
  local copies, waits for them, and re-layouts  3.38 us (6%)
  between operations  0.73 us (1%)
    pallas_call x1, Pallas kernels, on_device(): pl.pallas_call(functools.partial(layer_kernel, Z), in_specs=[anywhere] *...  46.5 us
    pallas_call x1, Pallas kernels, dense_rows(): pl.pallas_call(dense_kernel, grid_spec=pltpu.PrefetchScalarGridSpec(num_s...  3.97 us
    unnamed x20, local copies, waits for them, and re-layouts  3.38 us
    pallas_call x1, Pallas kernels, on_device(): pl.pallas_call(finish_kernel, in_specs=[vmem] * 3, out_specs=[pl.BlockSpe...  1.93 us

profile of v2, /device:TPU:0, one launch (start us, length us, event | category | flops | bytes accessed | tf_op | source)
XLA Modules:
  0.0 56.5 jit_solution(17634710573400918683)
XLA Ops:
  0.6 0.0 copy-start.4
  0.6 0.0 copy-start.3
  0.7 0.0 copy-start.2
  0.7 0.0 copy-start.6
  0.7 0.7 %copy-done.6 = s32[2,64]{1,0:T(2,128)S(1)} copy-done((s32[2,64]{1,0:T(2,128)S(1)}, s32[2,64]{1,0:T(2,128)}, u32[]{:S(2)}) %copy-start.6) | copy-done | bytes 536
  1.4 0.0 copy-start.9
  1.4 0.7 %copy-done.9 = s32[2]{0:T(128)S(1)} copy-done((s32[2]{0:T(128)S(1)}, s32[2]{0:T(128)}, u32[]{:S(2)}) %copy-start.9) | copy-done | bytes 32
  2.0 0.0 copy-start.7
  2.0 0.0 copy-start.8
  2.1 4.0 %shard_map.111 = (bf16[16,256,256]{2,1,0:T(8,128)(2,1)S(1)}, f32[256,128]{1,0:T(8,128)S(1)}) custom-call(s32[2,64]{1,0:T(2,128)S(1)} %copy-done.6, s32[2]{0:T(128)S(1)} %copy-done.9, bf16[2,64,128,128]{3,2,1,0:T(8,128)(2,1)} %tiles_ref.1), custom_call_target="tpu_custom_call" | custom-call | tf_op jit(solution)/shard_map/pallas_call | solution.py:57
  6.0 0.0 copy-done.4
  6.0 0.0 copy-done.3
  6.0 0.0 copy-done.2
  6.1 0.0 copy-done.7
  6.1 0.0 copy-done.8
  6.1 46.5 %shard_map.112 = (f32[8,128]{1,0:T(8,128)S(1)}, bf16[2,256,256]{2,1,0:T(8,128)(2,1)S(1)}, f32[256,256]{1,0:T(8,128)S(1)}) custom-call(bf16[256,256]{1,0:T(8,128)(2,1)S(1)} %copy-done.2, bf16[256,256]{1,0:T(8,128)(2,1)S(1)} %copy-done.3, bf16[256,256]{1,0:T(8,128)(2,1)S(1)} %copy-done.4, bf16[8,2,256,256]{3,2,1,0:T(8,128)(2,1)S(1)} %bitcast.3, ...), custom_call_target="tpu_custom_call" | custom-call | tf_op jit(solution)/shard_map/pallas_call | solution.py:491
  52.5 0.0 copy-start
  52.6 0.7 %copy-done = bf16[2,256,256]{2,1,0:T(8,128)(2,1)} copy-done((bf16[2,256,256]{2,1,0:T(8,128)(2,1)}, bf16[2,256,256]{2,1,0:T(8,128)(2,1)S(1)}, u32[]{:S(2)}) %copy-start) | copy-done | bytes 262168
  53.3 0.0 copy-start.1
  53.3 0.7 %copy-done.1 = f32[256,256]{1,0:T(8,128)} copy-done((f32[256,256]{1,0:T(8,128)}, f32[256,256]{1,0:T(8,128)S(1)}, u32[]{:S(2)}) %copy-start.1) | copy-done | bytes 262168
  54.0 0.0 copy-start.5
  54.0 0.6 %copy-done.5 = f32[8,128]{1,0:T(8,128)} copy-done((f32[8,128]{1,0:T(8,128)}, f32[8,128]{1,0:T(8,128)S(1)}, u32[]{:S(2)}) %copy-start.5) | copy-done | bytes 4120
  54.5 1.9 %shard_map.113 = (f32[1]{0:T(128)}, f32[256,256]{1,0:T(8,128)}, f32[256,256]{1,0:T(8,128)}, f32[256,256]{1,0:T(8,128)}) custom-call(f32[8,128]{1,0:T(8,128)} %copy-done.5, bf16[2,256,256]{2,1,0:T(8,128)(2,1)} %copy-done, f32[256,256]{1,0:T(8,128)} %copy-done.1), custom_call_target="tpu_custom_call" | custom-call | tf_op jit(solution)/shard_map/pallas_call | solution.py:544
Async XLA Ops:
  0.6 5.4 %copy-start.4 = (bf16[256,256]{1,0:T(8,128)(2,1)S(1)}, bf16[256,256]{1,0:T(8,128)(2,1)}, u32[]{:S(2)}) copy-start(bf16[256,256]{1,0:T(8,128)(2,1)} %wn_hbm.1) | copy-start | bytes 393220
  0.6 5.4 %copy-start.3 = (bf16[256,256]{1,0:T(8,128)(2,1)S(1)}, bf16[256,256]{1,0:T(8,128)(2,1)}, u32[]{:S(2)}) copy-start(bf16[256,256]{1,0:T(8,128)(2,1)} %ws_hbm.1) | copy-start | bytes 393220
  0.7 5.4 %copy-start.2 = (bf16[256,256]{1,0:T(8,128)(2,1)S(1)}, bf16[256,256]{1,0:T(8,128)(2,1)}, u32[]{:S(2)}) copy-start(bf16[256,256]{1,0:T(8,128)(2,1)} %x_hbm.1) | copy-start | bytes 393220
  0.7 0.7 %copy-start.6 = (s32[2,64]{1,0:T(2,128)S(1)}, s32[2,64]{1,0:T(2,128)}, u32[]{:S(2)}) copy-start(s32[2,64]{1,0:T(2,128)} %cols_ref.1) | copy-start | bytes 1540
  1.4 0.7 %copy-start.9 = (s32[2]{0:T(128)S(1)}, s32[2]{0:T(128)}, u32[]{:S(2)}) copy-start(s32[2]{0:T(128)} %count_ref.1) | copy-start | bytes 28
  2.0 4.0 %copy-start.7 = (s32[256]{0:T(256)S(1)}, s32[256]{0:T(256)}, u32[]{:S(2)}) copy-start(s32[256]{0:T(256)} %param.14) | copy-start | bytes 3076
  2.0 4.0 %copy-start.8 = (s32[256]{0:T(256)S(1)}, s32[256]{0:T(256)}, u32[]{:S(2)}) copy-start(s32[256]{0:T(256)} %param.15) | copy-start | bytes 3076
  52.5 0.7 %copy-start = (bf16[2,256,256]{2,1,0:T(8,128)(2,1)}, bf16[2,256,256]{2,1,0:T(8,128)(2,1)S(1)}, u32[]{:S(2)}) copy-start(bf16[2,256,256]{2,1,0:T(8,128)(2,1)S(1)} %get-tuple-element.12.grads_ref) | copy-start | bytes 786436
  53.3 0.7 %copy-start.1 = (f32[256,256]{1,0:T(8,128)}, f32[256,256]{1,0:T(8,128)S(1)}, u32[]{:S(2)}) copy-start(f32[256,256]{1,0:T(8,128)S(1)} %get-tuple-element.13.gfeat_ref) | copy-start | bytes 786436
  54.0 0.6 %copy-start.5 = (f32[8,128]{1,0:T(8,128)}, f32[8,128]{1,0:T(8,128)S(1)}, u32[]{:S(2)}) copy-start(f32[8,128]{1,0:T(8,128)S(1)} %get-tuple-element.11.loss_ref) | copy-start | bytes 12292
